TPU v7x, 256 devices: a whole 4x4x8 slice. The times are simulated.
256 devices in a mesh: mode: 8 (over z_hi, y), space: 32 (over x, z_lo, core).
Axes of the slice: x: 4, y: 4, z: 8 (z_hi: 2, z_lo: 4; z = z_hi * 4 + z_lo), core: 2. Of those that a mesh axis runs over, the one named last changes fastest.
Arguments:
- energy: float32 [128, 256, 16, 128], P('mode', 'space'), may hold values from -6 to 6
- void: int32 [256, 16, 128], P('space'), may hold values 0 or 1
- spacing_cells: float32 [256, 16, 128], P('space'), may hold values from 2 to 50
- walls: int32 [2, 256, 128], P(None, 'space'), may hold values from 0 to 2
- octant: int32 [128], replicated, may hold values from 0 to 7
- specific_warmth_modes: float32 [128], replicated, may hold values from 0.2 to 2
- second_derivative: float32 [128], replicated, may hold values from 0.5 to 1.5
- umklapp: float32 [128], replicated, may hold values from 0.02 to 1
- isotope: float32 [128], replicated, may hold values from 0.01 to 0.3
- courant: float32 [3, 128], replicated, may hold values from 0.05 to 0.9
Outputs:
- final_energy: float32 [128, 256, 16, 128], P('mode', 'space')
- prior_pseudo_kelvin: float32 [256, 16, 128], P('space')
Inputs may be any that keep to these rules, and one draw needn't show every extreme that they name: `walls`: 0 adiabatic wall, 1 cold black wall, 2 hot black wall. `octant`: bit 0, 1 and 2 give a negative direction along the first, second and third dimension.
All inputs are finite; a program needn't handle non-finite values. No bound on the sum of `void` on one device may be relied on, other than what follows from the above.
Results may differ from a plain program's by a relative error of at most 0.0003.
Values sent between devices are 32-bit elements; how exact they have to be, the bound alone decides.
A program may use at most 64 MiB of HBM per device.

v0:
```python
import jax
import jax.numpy as jnp
from jax import lax
from jax.sharding import PartitionSpec as P

ITERS = 8


RELAX_WEIGHT = 0.35
HOT_WALL = 1.0


def with_halo(cells, sides, width):
    for axis, dim in sides:
        count = lax.axis_size(axis)
        head = lax.slice_in_dim(cells, 0, width, axis=dim)
        tail = lax.slice_in_dim(cells, cells.shape[dim] - width, cells.shape[dim], axis=dim)
        cells = jnp.concatenate(
            [
                lax.ppermute(tail, axis, [(i, (i + 1) % count) for i in range(count)]),
                cells,
                lax.ppermute(head, axis, [((i + 1) % count, i) for i in range(count)]),
            ],
            axis=dim,
        )
    return cells


def broadcast_modes(vector):
    return vector[:, None, None, None]


def mode_signs(octant):
    sign_x = 1 - 2 * (octant % 2)
    sign_y = 1 - 2 * (octant // 2 % 2)
    sign_z = 1 - 2 * (octant // 4)
    return (sign_x, sign_y, sign_z)


def transfer_rate(umklapp, isotope, speed, spacing_cells):
    rate = broadcast_modes(umklapp + isotope) + broadcast_modes(speed) / spacing_cells[None]
    return 1.0 - jnp.exp(-rate)


def rest_population(specific_warmth_modes, second_derivative, prior_pseudo_kelvin):
    weighted_quantity = broadcast_modes(second_derivative) * prior_pseudo_kelvin[None]
    return (
        broadcast_modes(specific_warmth_modes / second_derivative) * jnp.sinh(weighted_quantity),
        broadcast_modes(specific_warmth_modes) * jnp.cosh(weighted_quantity),
    )


def beam_update(field, near, far, courant_band):
    factor = broadcast_modes(courant_band)
    return (
        field
        - 0.5 * factor * (3.0 * field - 4.0 * near + far)
        + 0.5 * factor * factor * (field - 2.0 * near + far)
    )


def beam_rolled(field, courant_band, sign, axis):
    forward = broadcast_modes(sign) > 0
    near = jnp.where(forward, jnp.roll(field, 1, axis), jnp.roll(field, -1, axis))
    far = jnp.where(forward, jnp.roll(field, 2, axis), jnp.roll(field, -2, axis))
    return beam_update(field, near, far, courant_band)


def wall_sweep(field, courant_band, sign, walls, specific_warmth_modes, second_derivative):
    factor = broadcast_modes(courant_band)
    forward = broadcast_modes(sign) > 0
    inflow = broadcast_modes(
        specific_warmth_modes / second_derivative * jnp.sinh(second_derivative * HOT_WALL)
    )
    bottom = jnp.where(walls[0] == 2, 1.0, 0.0)[None, :, None, :] * inflow
    upper = jnp.where(walls[1] == 2, 1.0, 0.0)[None, :, None, :] * inflow
    from_below = jnp.concatenate([bottom, field[:, :, :-1]], axis=2)
    from_above = jnp.concatenate([field[:, :, 1:], upper], axis=2)
    upstream = jnp.where(forward, from_below, from_above)
    depth = lax.broadcasted_iota(jnp.int32, (1, 1, field.shape[2], 1), 2)
    block_top = (depth == field.shape[2] - 1) & (walls[1] == 0)[None, :, None, :]
    block_bottom = (depth == 0) & (walls[0] == 0)[None, :, None, :]
    blocked = jnp.where(forward, block_top, block_bottom)
    outflow = jnp.where(blocked, 0.0, factor * field)
    return field - outflow + factor * upstream


def local(
    energy,
    void,
    spacing_cells,
    walls,
    octant,
    specific_warmth_modes,
    second_derivative,
    umklapp,
    isotope,
    courant,
):
    band_count = energy.shape[0]
    first_band = lax.axis_index("mode") * band_count

    def own_bands(table):
        return lax.dynamic_slice_in_dim(table, first_band, band_count, table.ndim - 1)

    fluid = (1 - void).astype(jnp.float32)
    sign_x, sign_y, sign_z = mode_signs(own_bands(octant))
    speed_all = jnp.sqrt(jnp.sum(courant * courant, axis=0))
    local_specific_warmth = own_bands(specific_warmth_modes)
    local_second_derivative = own_bands(second_derivative)
    own_courant = own_bands(courant)
    relax = transfer_rate(
        own_bands(umklapp), own_bands(isotope), own_bands(speed_all), spacing_cells
    )
    iterate_carry = energy * fluid[None]
    prior_pseudo_kelvin = jnp.zeros(spacing_cells.shape, jnp.float32)
    for sweep in range(ITERS):
        matrix_element, derivative_of_content = rest_population(
            local_specific_warmth, local_second_derivative, prior_pseudo_kelvin
        )
        balance_mismatch, combined_derivative = lax.psum(
            (
                jnp.sum(relax * (matrix_element - iterate_carry), axis=0),
                jnp.sum(relax * derivative_of_content, axis=0),
            ),
            "mode",
        )
        prior_pseudo_kelvin = (
            prior_pseudo_kelvin - RELAX_WEIGHT * balance_mismatch / combined_derivative
        )
    matrix_element, derivative_of_content = rest_population(
        local_specific_warmth, local_second_derivative, prior_pseudo_kelvin
    )
    iterate_carry = iterate_carry + relax * (matrix_element - iterate_carry)
    padded = with_halo(iterate_carry, (("space", 1),), 2)
    width = iterate_carry.shape[1]
    forward = broadcast_modes(sign_x) > 0
    near = jnp.where(forward, padded[:, 1 : 1 + width], padded[:, 3 : 3 + width])
    far = jnp.where(forward, padded[:, 0:width], padded[:, 4 : 4 + width])
    iterate_carry = beam_update(iterate_carry, near, far, own_courant[0])
    iterate_carry = wall_sweep(
        iterate_carry, own_courant[2], sign_z, walls, local_specific_warmth, local_second_derivative
    )
    iterate_carry = beam_rolled(iterate_carry, own_courant[1], sign_y, 3)
    iterate_carry = iterate_carry * fluid[None]
    return (iterate_carry, prior_pseudo_kelvin)


def solution(mesh):
    in_specs = (
        P("mode", "space", None, None),
        P("space", None, None),
        P("space", None, None),
        P(None, "space", None),
        P(),
        P(),
        P(),
        P(),
        P(),
        P(),
    )
    out_specs = (P("mode", "space", None, None), P("space", None, None))
    return jax.shard_map(local, mesh=mesh, in_specs=in_specs, out_specs=out_specs, check_vma=False)
```

profile of v0, /device:TPU:38, one launch (start us, length us, event | category | flops | bytes accessed | tf_op | source)
XLA Modules:
  0.0 876.8 jit_solution(9419108738488289381)
XLA Ops:
  7.2 0.8 multiply_reduce_fusion.2
  8.0 0.1 dynamic_slice.23
  8.1 0.8 fusion.150
  8.9 0.8 subtract_convert_fusion
  9.8 2.4 multiply_reduce_fusion.1
  12.2 0.0 all-reduce.29.cloned.1.call-start
  12.3 108.1 %all-reduce.31.cloned.1.call-done = (f32[8,16,128]{2,1,0:T(8,128)}, f32[8,16,128]{2,1,0:T(8,128)}) async-done(((f32[8,16,128]{2,1,0:T(8,128)}, f32[8,16,128]{2,1,0:T(8,128)}), (f32[8,16,128]{2,1,0:T(8,128)}, f32[8,16,128]{2,1,0:T(8,128)})) %all-reduce.31.cloned.1.call-update) | async-done | bytes 131088 | tf_op jit(solution)/shard_map/psum | solution.py:121
  120.3 0.9 divide_subtract_fusion.7
  121.3 2.1 fusion.140
  123.4 0.0 all-reduce.27.cloned.1.call-start
  123.5 101.9 %all-reduce.29.cloned.1.call-done = (f32[8,16,128]{2,1,0:T(8,128)}, f32[8,16,128]{2,1,0:T(8,128)}) async-done(((f32[8,16,128]{2,1,0:T(8,128)}, f32[8,16,128]{2,1,0:T(8,128)}), (f32[8,16,128]{2,1,0:T(8,128)}, f32[8,16,128]{2,1,0:T(8,128)})) %all-reduce.29.cloned.1.call-update) | async-done | bytes 131088 | tf_op jit(solution)/shard_map/psum | solution.py:121
  225.4 0.9 divide_subtract_fusion.6
  226.3 2.1 fusion.139
  228.5 101.8 %all-reduce.27.cloned.1.call-done = (f32[8,16,128]{2,1,0:T(8,128)}, f32[8,16,128]{2,1,0:T(8,128)}) async-done(((f32[8,16,128]{2,1,0:T(8,128)}, f32[8,16,128]{2,1,0:T(8,128)}), (f32[8,16,128]{2,1,0:T(8,128)}, f32[8,16,128]{2,1,0:T(8,128)})) %all-reduce.27.cloned.1.call-update) | async-done | bytes 131088 | tf_op jit(solution)/shard_map/psum | solution.py:121
  330.4 0.9 divide_subtract_fusion.5
  331.3 2.1 fusion.138
  333.5 101.8 %all-reduce.25.cloned.1.call-done = (f32[8,16,128]{2,1,0:T(8,128)}, f32[8,16,128]{2,1,0:T(8,128)}) async-done(((f32[8,16,128]{2,1,0:T(8,128)}, f32[8,16,128]{2,1,0:T(8,128)}), (f32[8,16,128]{2,1,0:T(8,128)}, f32[8,16,128]{2,1,0:T(8,128)})) %all-reduce.25.cloned.1.call-update) | async-done | bytes 131088 | tf_op jit(solution)/shard_map/psum | solution.py:121
  435.3 0.9 divide_subtract_fusion.4
  436.2 2.1 fusion.137
  438.4 0.1 broadcast_and_fusion
  438.5 101.7 %all-reduce.23.cloned.1.call-done = (f32[8,16,128]{2,1,0:T(8,128)}, f32[8,16,128]{2,1,0:T(8,128)}) async-done(((f32[8,16,128]{2,1,0:T(8,128)}, f32[8,16,128]{2,1,0:T(8,128)}), (f32[8,16,128]{2,1,0:T(8,128)}, f32[8,16,128]{2,1,0:T(8,128)})) %all-reduce.23.cloned.1.call-update) | async-done | bytes 131088 | tf_op jit(solution)/shard_map/psum | solution.py:121
  540.2 0.9 divide_subtract_fusion.3
  541.1 2.1 fusion.136
  543.3 0.1 constant_dynamic-slice_fusion
  543.4 101.7 %all-reduce.21.cloned.1.call-done = (f32[8,16,128]{2,1,0:T(8,128)}, f32[8,16,128]{2,1,0:T(8,128)}) async-done(((f32[8,16,128]{2,1,0:T(8,128)}, f32[8,16,128]{2,1,0:T(8,128)}), (f32[8,16,128]{2,1,0:T(8,128)}, f32[8,16,128]{2,1,0:T(8,128)})) %all-reduce.21.cloned.1.call-update) | async-done | bytes 131088 | tf_op jit(solution)/shard_map/psum | solution.py:121
  645.1 0.9 divide_subtract_fusion.2
  646.0 2.1 fusion.135
  648.1 0.2 all-reduce.17.cloned.1.call-start
  648.4 101.7 %all-reduce.19.cloned.1.call-done = (f32[8,16,128]{2,1,0:T(8,128)}, f32[8,16,128]{2,1,0:T(8,128)}) async-done(((f32[8,16,128]{2,1,0:T(8,128)}, f32[8,16,128]{2,1,0:T(8,128)}), (f32[8,16,128]{2,1,0:T(8,128)}, f32[8,16,128]{2,1,0:T(8,128)})) %all-reduce.19.cloned.1.call-update) | async-done | bytes 131088 | tf_op jit(solution)/shard_map/psum | solution.py:121
  750.0 0.9 divide_subtract_fusion.1
  750.9 2.1 fusion.134
  753.1 0.1 fusion.148
  753.2 101.8 %all-reduce.17.cloned.1.call-done = (f32[8,16,128]{2,1,0:T(8,128)}, f32[8,16,128]{2,1,0:T(8,128)}) async-done(((f32[8,16,128]{2,1,0:T(8,128)}, f32[8,16,128]{2,1,0:T(8,128)}), (f32[8,16,128]{2,1,0:T(8,128)}, f32[8,16,128]{2,1,0:T(8,128)})) %all-reduce.17.cloned.1.call-update) | async-done | bytes 131088 | tf_op jit(solution)/shard_map/psum | solution.py:121
  855.1 0.9 divide_subtract_fusion
  856.0 1.3 fusion.130
  857.4 0.1 collective-permute-start
  857.5 1.7 collective-permute-start.1
  859.2 0.1 broadcast_multiply_fusion
  859.3 3.9 collective-permute-done
  863.2 1.7 collective-permute-done.1
  865.0 0.6 multiply_add_fusion.8
  865.5 0.2 fusion.156
  865.7 0.5 fusion.133
  866.3 0.4 fusion.155
  866.7 0.4 fusion.154
  867.0 0.4 fusion.153
  867.4 0.4 fusion.152
  867.8 2.2 add_multiply_fusion
  (36 shorter events, 0.5 us)
Async XLA Ops:
  7.2 114.1 %copy-start.1 = (f32[8,16,128]{2,1,0:T(8,128)S(1)}, f32[8,16,128]{2,1,0:T(8,128)}, u32[]{:S(2)}) copy-start(f32[8,16,128]{2,1,0:T(8,128)} %param.12) | copy-start | bytes 196612
  7.2 114.1 %copy-start = (f32[16,8,16,128]{3,2,1,0:T(8,128)S(1)}, f32[16,8,16,128]{3,2,1,0:T(8,128)}, u32[]{:S(2)}) copy-start(f32[16,8,16,128]{3,2,1,0:T(8,128)} %param.10) | copy-start | bytes 3145732
  7.2 113.2 %all-reduce.31.cloned.1.call-start = ((), (), s32[]{:S(2)}) async-start(), calls=%async_computation.7 | async-start | bytes 262144 | tf_op jit(solution)/shard_map/psum | solution.py:121
  12.2 213.2 %all-reduce.29.cloned.1.call-start = ((), (), s32[]{:S(2)}) async-start(), calls=%async_computation.6 | async-start | bytes 262144 | tf_op jit(solution)/shard_map/psum | solution.py:121
  123.4 206.9 %all-reduce.27.cloned.1.call-start = ((), (), s32[]{:S(2)}) async-start(), calls=%async_computation.5 | async-start | bytes 262144 | tf_op jit(solution)/shard_map/psum | solution.py:121
  226.3 2.2 copy-start.3
  228.5 206.8 %all-reduce.25.cloned.1.call-start = ((), (), s32[]{:S(2)}) async-start(), calls=%async_computation.4 | async-start | bytes 262144 | tf_op jit(solution)/shard_map/psum | solution.py:121
  333.4 206.8 %all-reduce.23.cloned.1.call-start = ((), (), s32[]{:S(2)}) async-start(), calls=%async_computation.3 | async-start | bytes 262144 | tf_op jit(solution)/shard_map/psum | solution.py:121
  438.3 206.8 %all-reduce.21.cloned.1.call-start = ((), (), s32[]{:S(2)}) async-start(), calls=%async_computation.2 | async-start | bytes 262144 | tf_op jit(solution)/shard_map/psum | solution.py:121
  541.1 2.2 copy-start.4
  543.3 206.8 %all-reduce.19.cloned.1.call-start = ((), (), s32[]{:S(2)}) async-start(), calls=%async_computation.1 | async-start | bytes 262144 | tf_op jit(solution)/shard_map/psum | solution.py:121
  648.1 206.9 %all-reduce.17.cloned.1.call-start = ((), (), s32[]{:S(2)}) async-start(), calls=%async_computation | async-start | bytes 262144 | tf_op jit(solution)/shard_map/psum | solution.py:121
  750.9 2.2 copy-start.5
  856.0 1.3 copy-start.2
  857.4 5.9 collective-permute-start
  857.5 7.5 collective-permute-start.1
Sparse Core Ops, SparseCore 0:
  12.3 107.9 all-reduce.30
  123.8 101.5 all-reduce.28
  228.6 101.6 all-reduce.26
  333.6 101.5 all-reduce.24
  438.4 101.6 all-reduce.22
  543.5 101.5 all-reduce.20
  648.3 101.6 all-reduce.18
  753.5 101.5 all-reduce.16
where the time goes:
time: 881 us; the launch traced here: 877 us
  waiting for transfers between devices  826 us (94%)
  other arithmetic  31.9 us (4%)
  between operations  14.4 us (2%)
    psum x8, waiting for transfers between devices, local(): lax.psum((jnp.sum(relax * (matrix_element - iterate_carry), axis=0), jnp....  820 us
  transfers between devices with their start and end apart: 10, of which 10 were waited for; matrix products, arithmetic and copies ran while one was open for 0% of the time, Pallas kernels for 0%

commit v1 on v0

v1 whole, which is shorter than its diff:
```python
import functools
import math

import jax
import jax.numpy as jnp
from jax import lax
from jax.experimental import pallas as pl
from jax.experimental.pallas import tpu as pltpu
from jax.sharding import PartitionSpec as P

MESH = pl.DeviceIdType.MESH
ITERS = 8
RELAX_WEIGHT = 0.35
HOT_WALL = 1.0
TERMS = 22
RATE_TERMS = 12
SCALE = 8.0
F32 = jnp.float32

(N_RATE, N_SPEED, WARM_HALF, CURVE, GO_X, GO_Y, GO_Z, X0, X1, X2, CZ, Y0, Y1, Y2, HOT) = range(15)


def sweep_factors(c):
    return 1.0 - 1.5 * c + 0.5 * c * c, 2.0 * c - c * c, 0.5 * c * c - 0.5 * c


def kernel(
    space,
    energy, void, spacing, walls, octant, warmth, curve, umklapp, isotope, courant,
    out, temp_out,
    st, sp, vd, wl, oc, pv, cr, fl, up_keep, dn_keep, bot, top,
    part, got, mu, zt, tab, uu, ww, tp, res,
    in_sem, small_sem, rs_send, rs_recv, t_send, t_recv, h_send, h_recv, out_sem, l_sem, g_sem, go_sem,
):
    m, s = lax.axis_index("mode"), lax.axis_index("space")
    left, right = lax.rem(s + space - 1, space), lax.rem(s + 1, space)
    y = lax.rem(m, 4)
    early = m < 4
    late = m >= 4

    def signal(sem, mode, strip):
        pl.semaphore_signal(sem, inc=1, device_id=(mode, strip), device_id_type=MESH)

    small = [
        pltpu.make_async_copy(src, dst, small_sem.at[i])
        for i, (src, dst) in enumerate(
            (
                (spacing, sp.at[pl.ds(2, 8)]),
                (void, vd),
                (umklapp, pv.at[pl.ds(0, 1)]),
                (isotope, pv.at[pl.ds(8, 1)]),
                (courant, cr),
                (warmth, pv.at[pl.ds(16, 1)]),
                (curve, pv.at[pl.ds(24, 1)]),
                (octant, oc),
                (walls, wl),
            )
        )
    ]
    loads = [
        pltpu.make_async_copy(
            energy.at[:, pl.ds(4 * i, 4)], st.at[:, pl.ds(2 + 4 * i, 4)], in_sem.at[i]
        )
        for i in range(2)
    ]
    for c in small[:5]:
        c.start()
    for c in loads:
        c.start()
    for c in small[5:]:
        c.start()

    barrier = pltpu.get_barrier_semaphore()

    @pl.when(early)
    def _():
        for j in range(1, 8):
            signal(barrier, lax.rem(m + j, 8), s)
        for strip in (left, right):
            signal(barrier, y, strip)
            signal(barrier, 4 + y, strip)

    @pl.when(m == 0)
    def _():
        for k in range(8):
            signal(barrier, k, left)

    @pl.when(m == 2)
    def _():
        for k in range(8):
            signal(barrier, k, right)

    for c in small[:5]:
        c.wait()

    lane = lax.broadcasted_iota(jnp.int32, (16, 128), 1)
    band = lax.broadcasted_iota(jnp.int32, (16, 128), 0) + 16 * m

    def own(vector):
        picked = jnp.where(lane == band, jnp.broadcast_to(vector, (16, 128)), 0.0)
        return jnp.broadcast_to(jnp.sum(picked, axis=1, keepdims=True), (16, 128))

    rate = pv[0:1, :] + pv[8:9, :]
    cx, cy, cz = cr[0:1, :], cr[1:2, :], cr[2:3, :]
    speed = jnp.sqrt(cx * cx + cy * cy + cz * cz)
    tab[N_RATE] = own(-rate)
    tab[N_SPEED] = own(-speed)

    pl.semaphore_wait(barrier, jnp.where(early, 7, 8))

    @pl.when(late)
    def _():
        for strip in (s, left, right):
            signal(g_sem, y, strip)
        for k in range(4):
            signal(l_sem, k, s)

    def row(table, b):
        return tab[table, pl.ds(b, 1), :]

    def pass_one(r, carry):
        inverse = 1.0 / sp[2 + r]
        total = jnp.zeros((16, 128), F32)
        for b in range(16):
            kept = jnp.exp(row(N_RATE, b) + row(N_SPEED, b) * inverse)
            total = total + (1.0 - kept) * st[b, 2 + r]
        fluid = (1 - vd[r]).astype(F32)
        fl[r] = fluid
        part[r] = total * fluid
        return carry

    sends = []

    def send(first, count, mode, strip, i, when):
        c = pltpu.make_async_remote_copy(
            part.at[pl.ds(first, count)],
            got.at[m, pl.ds(0, count)],
            rs_send.at[i],
            rs_recv.at[m],
            device_id=(mode, strip),
            device_id_type=MESH,
        )
        sends.append((c, when))
        if when is None:
            c.start()
        else:
            pl.when(when)(c.start)

    loads[0].wait()
    lax.fori_loop(0, 4, pass_one, 0)
    send(0, 4, 1, s, 0, m != 1)
    send(0, 2, 2, left, 1, None)
    loads[1].wait()
    lax.fori_loop(4, 8, pass_one, 0)
    send(4, 4, 3, s, 2, m != 3)
    send(6, 2, 0, right, 3, None)

    @pl.when(m == 1)
    def _():
        got[1] = part[0:4]

    @pl.when(m == 3)
    def _():
        got[3] = part[4:8]

    for c in small[5:]:
        c.wait()

    warm, bend = pv[16:17, :], pv[24:25, :]
    own_warm, own_bend = own(warm), own(bend)
    tab[WARM_HALF] = 0.5 * own_warm / own_bend
    tab[CURVE] = own_bend
    tab[HOT] = (0.5 * own_warm / own_bend) * (jnp.exp(own_bend * HOT_WALL) - jnp.exp(-own_bend * HOT_WALL))
    octants = own(oc[0:1, :].astype(F32)).astype(jnp.int32)
    tab[GO_X] = (1 - lax.rem(octants, 2)).astype(F32)
    tab[GO_Y] = (1 - lax.rem(octants // 2, 2)).astype(F32)
    tab[GO_Z] = (1 - octants // 4).astype(F32)
    tab[X0], tab[X1], tab[X2] = sweep_factors(own(cx))
    tab[Y0], tab[Y1], tab[Y2] = sweep_factors(own(cy))
    tab[CZ] = own(cz)

    def weights(p, b, held, inverse):
        kept = jnp.exp(row(N_RATE, b) + row(N_SPEED, b) * inverse)
        uu[b, p] = kept * held
        ww[b, p] = (1.0 - kept) * row(WARM_HALF, b)

    def pass_two(r, carry):
        inverse = 1.0 / sp[2 + r]
        fluid = fl[r]
        for b in range(16):
            held = st[b, 2 + r] * fluid
            st[b, 2 + r] = held
            weights(2 + r, b, held, inverse)
        return carry

    lax.fori_loop(0, 8, pass_two, 0)

    halos = []
    for i, (src, dst, strip) in enumerate(((8, 0, right), (2, 10, left))):
        for j, (a, b) in enumerate(
            (
                (sp.at[pl.ds(src, 2)], sp.at[pl.ds(dst, 2)]),
                (st.at[:, pl.ds(src, 2)], st.at[:, pl.ds(dst, 2)]),
            )
        ):
            halos.append(
                pltpu.make_async_remote_copy(
                    a, b, h_send.at[2 * i + j], h_recv.at[2 * i + j], device_id=(m, strip), device_id_type=MESH
                )
            )

    @pl.when(early)
    def _():
        for c in halos:
            c.start()

    depth = lax.broadcasted_iota(jnp.int32, (16, 128), 0)

    def wall_rows(r, carry):
        low = jnp.broadcast_to(wl[0, pl.ds(r, 1), :], (16, 128))
        high = jnp.broadcast_to(wl[1, pl.ds(r, 1), :], (16, 128))
        up_keep[r] = jnp.where((depth == 15) & (high == 0), 0.0, 1.0)
        dn_keep[r] = jnp.where((depth == 0) & (low == 0), 0.0, 1.0)
        bot[r] = jnp.where((depth == 0) & (low == 2), 1.0, 0.0)
        top[r] = jnp.where((depth == 15) & (high == 2), 1.0, 0.0)
        return carry

    lax.fori_loop(0, 8, wall_rows, 0)

    def series():
        order = lax.broadcasted_iota(jnp.int32, (16, 128), 0)
        rest = jnp.exp(-rate)
        powers = jnp.zeros((16, 128), F32)
        term = -rest
        for j in range(RATE_TERMS):
            value = 1.0 - rest if j == 0 else term
            powers = jnp.where(order == j, jnp.broadcast_to(value, (16, 128)), powers)
            term = term * (-speed) * (1.0 / (j + 1))
        weight = warm
        for k in range(TERMS):
            summed = jnp.sum(powers * weight, axis=1, keepdims=True)
            zt[k] = jnp.broadcast_to(summed, (16, 128))
            weight = weight * (bend * bend) * (SCALE * SCALE / ((2 * k + 2) * (2 * k + 3)))

    def moments(p, i):
        inverse = 1.0 / sp[p]
        for k in range(TERMS):
            value = jnp.broadcast_to(zt[k, RATE_TERMS - 1 : RATE_TERMS, :], (16, 128))
            for j in range(RATE_TERMS - 2, -1, -1):
                value = value * inverse + zt[k, j : j + 1, :]
            mu[k, i] = value

    def own_rows(base, count, peers):
        def one(i, carry):
            moments(base + i, i)
            return carry

        lax.fori_loop(0, count, one, 0)
        pl.semaphore_wait(g_sem, 3)
        signal(go_sem, 4 + y, s)
        for k in peers:
            pltpu.make_async_remote_copy(
                part.at[pl.ds(0, count)], got.at[k, pl.ds(0, count)], rs_send.at[0], rs_recv.at[k],
                device_id=(m, s), device_id_type=MESH,
            ).wait_recv()
        total = got[0, 0:count]
        for k in range(1, 8):
            total = total + got[k, 0:count]
        t = RELAX_WEIGHT * total / mu[0, 0:count]

        def iterate(_, t):
            q = (t * (1.0 / SCALE)) * (t * (1.0 / SCALE))
            value = mu[TERMS - 1, 0:count]
            slope = value
            for k in range(TERMS - 2, -1, -1):
                value = value * q + mu[k, 0:count]
                if k > 0:
                    slope = slope * q + value
            return t - RELAX_WEIGHT * (t * value - total) / (value + 2.0 * q * slope)

        t = lax.fori_loop(1, ITERS, iterate, t)
        tp[base : base + count] = t

    OWNED = {0: (0, 2), 1: (2, 4), 3: (6, 4), 2: (10, 2)}

    def t_copy(owner, mode, i):
        base, count = OWNED[owner]
        return pltpu.make_async_remote_copy(
            tp.at[pl.ds(base, count)], tp.at[pl.ds(base, count)], t_send.at[i], t_recv.at[owner],
            device_id=(mode, s), device_id_type=MESH,
        )

    pl.when(early)(series)
    for owner in range(4):
        @pl.when(m == owner)
        def _(owner=owner):
            base, count = OWNED[owner]
            if owner == 0:
                halos[0].wait_recv()
            if owner == 2:
                halos[2].wait_recv()
            own_rows(base, count, [k for k in range(8) if count == 2 or k != owner])
            for j in range(1, 4):
                t_copy(owner, (owner + j) % 4, j).start()
            pl.semaphore_wait(l_sem, 4)
            for j in range(4):
                t_copy(owner, 4 + j, 4 + j).start()

    @pl.when(late)
    def _():
        pl.semaphore_wait(go_sem, 1)
        for c in halos:
            c.start()

    def halo_rows(first):
        for p in (first, first + 1):
            inverse = 1.0 / sp[p]
            for b in range(16):
                weights(p, b, st[b, p], inverse)

    for i, c in enumerate(halos):
        if i == 0:
            pl.when(m != 0)(c.wait_recv)
        elif i == 2:
            pl.when(m != 2)(c.wait_recv)
        else:
            c.wait_recv()
            halo_rows((0, 10)[i // 2])

    for owner in range(4):
        pl.when(m != owner)(t_copy(owner, owner, 0).wait_recv)

    def relaxed(p, b, bend):
        x = tp[p] * bend
        return uu[b, p] + ww[b, p] * (jnp.exp(x) - jnp.exp(-x))

    def sweep(b, carry):
        bend = row(CURVE, b)
        go_x = jnp.broadcast_to(row(GO_X, b), (16, 128)) > 0.5
        go_y = jnp.broadcast_to(row(GO_Y, b), (16, 128)) > 0.5
        go_z = jnp.broadcast_to(row(GO_Z, b), (16, 128)) > 0.5
        inflow = jnp.where(go_z, depth, 15 - depth) == 0
        cells = {p: relaxed(p, b, bend) for p in range(2, 10)}
        for p, q in ((1, 10), (0, 11)):
            x = jnp.where(go_x, tp[p], tp[q]) * bend
            cells[p] = cells[q] = jnp.where(go_x, uu[b, p], uu[b, q]) + jnp.where(go_x, ww[b, p], ww[b, q]) * (
                jnp.exp(x) - jnp.exp(-x)
            )
        for r in range(8):
            p = r + 2
            near = jnp.where(go_x, cells[p - 1], cells[p + 1])
            far = jnp.where(go_x, cells[p - 2], cells[p + 2])
            a = row(X0, b) * cells[p] + row(X1, b) * near + row(X2, b) * far
            up = jnp.where(go_z, pltpu.roll(a, 1, 0), pltpu.roll(a, 15, 0))
            hot = jnp.where(go_z, bot[r], top[r]) * row(HOT, b)
            up = jnp.where(inflow, hot, up)
            keep = jnp.where(go_z, up_keep[r], dn_keep[r])
            a = a + row(CZ, b) * (up - keep * a)
            near = jnp.where(go_y, pltpu.roll(a, 1, 1), pltpu.roll(a, 127, 1))
            far = jnp.where(go_y, pltpu.roll(a, 2, 1), pltpu.roll(a, 126, 1))
            res[b, r] = (row(Y0, b) * a + row(Y1, b) * near + row(Y2, b) * far) * fl[r]
        pltpu.make_async_copy(res.at[b], out.at[b], out_sem.at[b]).start()
        return carry

    lax.fori_loop(0, 16, sweep, 0)
    last = pltpu.make_async_copy(tp.at[pl.ds(2, 8)], temp_out, out_sem.at[16])
    last.start()
    for b in range(16):
        pltpu.make_async_copy(res.at[b], out.at[b], out_sem.at[b]).wait()
    last.wait()
    for c, when in sends:
        if when is None:
            c.wait_send()
        else:
            pl.when(when)(c.wait_send)
    for c in halos:
        c.wait_send()
    for owner in range(4):
        @pl.when(m == owner)
        def _(owner=owner):
            for j in range(1, 8):
                t_copy(owner, owner, j).wait_send()


def solution(mesh):
    space = mesh.shape["space"]

    def local(energy, void, spacing, walls, octant, warmth, curve, umklapp, isotope, courant):
        flat = lambda v: v.reshape(1, 128)
        any_space = pl.BlockSpec(memory_space=pl.ANY)
        dma = pltpu.SemaphoreType.DMA
        regular = pltpu.SemaphoreType.REGULAR
        return pl.pallas_call(
            functools.partial(kernel, space),
            out_shape=(
                jax.ShapeDtypeStruct(energy.shape, F32),
                jax.ShapeDtypeStruct(spacing.shape, F32),
            ),
            in_specs=[pl.BlockSpec(memory_space=pltpu.HBM)] * 10,
            out_specs=(any_space, any_space),
            scratch_shapes=[
                pltpu.VMEM((16, 12, 16, 128), F32),
                pltpu.VMEM((12, 16, 128), F32),
                pltpu.VMEM((8, 16, 128), jnp.int32),
                pltpu.VMEM((2, 8, 128), jnp.int32),
                pltpu.VMEM((1, 128), jnp.int32),
                pltpu.VMEM((32, 128), F32),
                pltpu.VMEM((3, 128), F32),
            ]
            + [pltpu.VMEM((8, 16, 128), F32)] * 5
            + [
                pltpu.VMEM((8, 16, 128), F32),
                pltpu.VMEM((8, 4, 16, 128), F32),
                pltpu.VMEM((TERMS, 4, 16, 128), F32),
                pltpu.VMEM((TERMS, 16, 128), F32),
                pltpu.VMEM((15, 16, 128), F32),
                pltpu.VMEM((16, 12, 16, 128), F32),
                pltpu.VMEM((16, 12, 16, 128), F32),
                pltpu.VMEM((12, 16, 128), F32),
                pltpu.VMEM((16, 8, 16, 128), F32),
                dma((2,)),
                dma((9,)),
                dma((4,)),
                dma((8,)),
                dma((8,)),
                dma((4,)),
                dma((4,)),
                dma((4,)),
                dma((17,)),
                regular,
                regular,
                regular,
            ],
            compiler_params=pltpu.CompilerParams(
                collective_id=0, has_side_effects=True, vmem_limit_bytes=32 * 1024 * 1024
            ),
        )(
            *[
                pltpu.with_memory_space_constraint(v, pltpu.HBM)
                for v in (
                    energy, void, spacing, walls, flat(octant), flat(warmth), flat(curve), flat(umklapp),
                    flat(isotope), courant,
                )
            ]
        )

    in_specs = (
        P("mode", "space", None, None),
        P("space", None, None),
        P("space", None, None),
        P(None, "space", None),
        P(),
        P(),
        P(),
        P(),
        P(),
        P(),
    )
    out_specs = (P("mode", "space", None, None), P("space", None, None))
    return jax.shard_map(local, mesh=mesh, in_specs=in_specs, out_specs=out_specs, check_vma=False)
```

time: 881 us -> 29.7 us (0.03)
  the two profiles are of different devices: /device:TPU:38 before, /device:TPU:136 now
where the time goes in v1:
time: 29.7 us; the launch traced here: 29.6 us
  Pallas kernels  27.3 us (92%)
  local copies, waits for them, and re-layouts  1.6 us (5%)
  between operations  0.64 us (2%)
    pallas_call x1, Pallas kernels, local(): pl.pallas_call(functools.partial(kernel, space), out_shape=(jax.ShapeDtyp...  27.3 us
    unnamed x2, local copies, waits for them, and re-layouts  1.6 us

profile of v1, /device:TPU:136, one launch (start us, length us, event | category | flops | bytes accessed | tf_op | source)
XLA Modules:
  0.0 29.6 jit_solution(2012605983274525496)
XLA Ops:
  0.6 27.3 %shard_map.113 = (f32[16,8,16,128]{3,2,1,0:T(8,128)S(1)}, f32[8,16,128]{2,1,0:T(8,128)S(1)}) custom-call(f32[16,8,16,128]{3,2,1,0:T(8,128)} %energy.1, s32[8,16,128]{2,1,0:T(8,128)} %void.1, f32[8,16,128]{2,1,0:T(8,128)} %spacing.1, s32[2,8,128]{2,1,0:T(8,128)} %walls.1, s32[1,128]{1,0:T(1,128)} %bitcast.5, f32[1,128]{1,0:T(1,128)} %bitcast.6, ...), custom_call_target="tpu_custom_call" | custom-call | tf_op jit(solution)/shard_map/pallas_call | solution.py:393
  28.0 1.0 %copy.14 = f32[16,8,16,128]{3,2,1,0:T(8,128)} copy(f32[16,8,16,128]{3,2,1,0:T(8,128)S(1)} %get-tuple-element.4) | data formatting | bytes 2097152
  28.9 0.6 %copy.15 = f32[8,16,128]{2,1,0:T(8,128)} copy(f32[8,16,128]{2,1,0:T(8,128)S(1)} %get-tuple-element.5) | data formatting | bytes 131072

commit v2 on v1

v2 whole, which is shorter than its diff:
```python
import functools
import math

import jax
import jax.numpy as jnp
from jax import lax
from jax.experimental import pallas as pl
from jax.experimental.pallas import tpu as pltpu
from jax.sharding import PartitionSpec as P

MESH = pl.DeviceIdType.MESH
ITERS = 8
RELAX_WEIGHT = 0.35
HOT_WALL = 1.0
RUN = 8
TERMS = 22
RATE_TERMS = 12
SCALE = 8.0
F32 = jnp.float32

(N_RATE, N_SPEED, WARM_HALF, CURVE, GO_X, GO_Z, X0, X1, X2, CZ, Y0, Y1, Y2, HOT) = range(14)


def sweep_factors(c):
    return 1.0 - 1.5 * c + 0.5 * c * c, 2.0 * c - c * c, 0.5 * c * c - 0.5 * c


PIECES = ((0, 2, 2, 1, True), (1, 3, 0, 3, True), (2, 6, 0, 3, True), (3, 9, 0, 1, True), (0, 0, 0, 2, False), (3, 10, 1, 2, False))
INNER, OUTER = (2, 3, 4, 5), (0, 1, 6, 7)


def relaxed(t, held, pull, bend):
    x = t * bend
    return held + pull * (jnp.exp2(x) - jnp.exp2(-x))


def across(b, row, cells, rows, walls, state):
    up_keep, dn_keep, bot, top = walls
    depth = lax.broadcasted_iota(jnp.int32, (16, 128), 0)
    go_x = jnp.broadcast_to(row(GO_X, b), (16, 128)) > 0.5
    go_z = jnp.broadcast_to(row(GO_Z, b), (16, 128)) > 0.5
    inflow = jnp.where(go_z, depth, 15 - depth) == 0
    for i, r in enumerate(rows):
        p = r + 2
        near = jnp.where(go_x, cells[p - 1], cells[p + 1])
        far = jnp.where(go_x, cells[p - 2], cells[p + 2])
        a = row(X0, b) * cells[p] + row(X1, b) * near + row(X2, b) * far
        up = jnp.where(go_z, pltpu.roll(a, 1, 0), pltpu.roll(a, 15, 0))
        up = jnp.where(inflow, jnp.where(go_z, bot[r], top[r]) * row(HOT, b), up)
        keep = jnp.where(go_z, up_keep[r], dn_keep[r])
        state[b, i] = a + row(CZ, b) * (up - keep * a)


def along(b, row, octant, rows, fl, state, res):
    shift = jnp.where((octant & 2) == 0, 1, 127)
    twice = jnp.where((octant & 2) == 0, 2, 126)
    for i, r in enumerate(rows):
        a = state[b, i]
        near, far = pltpu.roll(a, shift, 1), pltpu.roll(a, twice, 1)
        res[b, i] = (row(Y0, b) * a + row(Y1, b) * near + row(Y2, b) * far) * fl[r]


def kernel(
    space,
    energy, void, spacing, walls, octant, warmth, curve, umklapp, isotope, courant,
    uu, ww, tp, fl, up_keep, dn_keep, bot, top, tab, oc, res,
    state, octants, st, sp, vd, wl, pv, cr, part, got, mu, zt,
    in_sem, small_sem, rs_send, rs_recv, own_recv, t_send, t_recv, h_send, h_recv, l_sem, left_sem, right_sem,
):
    m, s = lax.axis_index("mode"), lax.axis_index("space")
    left, right = lax.rem(s + space - 1, space), lax.rem(s + 1, space)
    y = lax.rem(m, 4)
    early = m < 4
    late = m >= 4

    def signal(sem, mode, strip):
        pl.semaphore_signal(sem, inc=1, device_id=(mode, strip), device_id_type=MESH)

    small = [
        pltpu.make_async_copy(src, dst, small_sem.at[i])
        for i, (src, dst) in enumerate(
            (
                (spacing, sp.at[pl.ds(2, 8)]),
                (void, vd),
                (umklapp, pv.at[pl.ds(0, 1)]),
                (isotope, pv.at[pl.ds(8, 1)]),
                (courant, cr),
                (warmth, pv.at[pl.ds(16, 1)]),
                (curve, pv.at[pl.ds(24, 1)]),
                (octant, oc),
                (walls, wl),
                (octant, octants),
            )
        )
    ]
    loads = [
        pltpu.make_async_copy(
            energy.at[:, pl.ds(4 * i, 4)], st.at[:, pl.ds(2 + 4 * i, 4)], in_sem.at[i]
        )
        for i in range(2)
    ]
    for c in small[:5]:
        c.start()
    for c in loads:
        c.start()
    for c in small[5:]:
        c.start()

    barrier = pltpu.get_barrier_semaphore()

    @pl.when(early)
    def _():
        for j in range(1, 8):
            signal(barrier, lax.rem(m + j, 8), s)
        for strip in (left, right):
            signal(barrier, y, strip)

    @pl.when(m == 0)
    def _():
        for k in range(8):
            signal(barrier, k, left)

    @pl.when(m == 3)
    def _():
        for k in range(8):
            signal(barrier, k, right)

    place = lax.rem(s, RUN)
    leads, trails = place == 0, place == RUN - 1

    @pl.when(late & ~trails)
    def _():
        signal(barrier, m, right)

    @pl.when(late & leads)
    def _():
        signal(barrier, m, left)

    for c in small[:5]:
        c.wait()

    lane = lax.broadcasted_iota(jnp.int32, (16, 128), 1)
    band = lax.broadcasted_iota(jnp.int32, (16, 128), 0) + 16 * m

    def own(vector):
        picked = jnp.where(lane == band, jnp.broadcast_to(vector, (16, 128)), 0.0)
        return jnp.broadcast_to(jnp.sum(picked, axis=1, keepdims=True), (16, 128))

    rate = pv[0:1, :] + pv[8:9, :]
    cx, cy, cz = cr[0:1, :], cr[1:2, :], cr[2:3, :]
    speed = jnp.sqrt(cx * cx + cy * cy + cz * cz)
    tab[N_RATE] = own(-rate)
    tab[N_SPEED] = own(-speed)

    pl.semaphore_wait(barrier, jnp.where(early, 7, 7 + trails.astype(jnp.int32) - leads.astype(jnp.int32)))

    @pl.when(late)
    def _():
        for k in range(4):
            signal(l_sem, k, s)

    @pl.when(late & ~leads)
    def _():
        signal(right_sem, m, left)

    @pl.when(late & trails)
    def _():
        signal(left_sem, m, right)

    def row(table, b):
        return tab[table, pl.ds(b, 1), :]

    def pass_one(r, carry):
        inverse = 1.0 / sp[2 + r]
        total = jnp.zeros((16, 128), F32)
        for b in range(16):
            kept = jnp.exp(row(N_RATE, b) + row(N_SPEED, b) * inverse)
            total = total + (1.0 - kept) * st[b, 2 + r]
        fluid = (1 - vd[r]).astype(F32)
        fl[r] = fluid
        part[r] = total * fluid
        return carry

    sends = []

    def send(first, count, slot, mode, strip, i, recv, when):
        c = pltpu.make_async_remote_copy(
            part.at[pl.ds(first, count)],
            got.at[m, pl.ds(slot, count)],
            rs_send.at[i],
            recv.at[m],
            device_id=(mode, strip),
            device_id_type=MESH,
        )
        sends.append((c, when))
        if when is None:
            c.start()
        else:
            pl.when(when)(c.start)

    loads[0].wait()
    lax.fori_loop(0, 4, pass_one, 0)
    send(0, 2, 1, 3, left, 0, rs_recv, None)
    send(1, 3, 0, 1, s, 1, rs_recv, m != 1)
    send(0, 1, 2, 0, s, 2, own_recv, m != 0)
    loads[1].wait()
    lax.fori_loop(4, 8, pass_one, 0)
    send(6, 2, 0, 0, right, 3, rs_recv, None)
    send(4, 3, 0, 2, s, 4, rs_recv, m != 2)
    send(7, 1, 0, 3, s, 5, own_recv, m != 3)

    for owner, slot, first, count in ((0, 2, 0, 1), (1, 0, 1, 3), (2, 0, 4, 3), (3, 0, 7, 1)):
        @pl.when(m == owner)
        def _(owner=owner, slot=slot, first=first, count=count):
            got[owner, slot : slot + count] = part[first : first + count]

    for c in small[5:]:
        c.wait()

    warm, bend = pv[16:17, :], pv[24:25, :]
    own_warm, own_bend = own(warm), own(bend)
    tab[WARM_HALF] = 0.5 * own_warm / own_bend
    tab[CURVE] = own_bend * (1.0 / math.log(2.0))
    tab[HOT] = (0.5 * own_warm / own_bend) * (jnp.exp(own_bend * HOT_WALL) - jnp.exp(-own_bend * HOT_WALL))
    codes = own(oc[0:1, :].astype(F32)).astype(jnp.int32)
    tab[GO_X] = 1.0 - (codes & 1).astype(F32)
    tab[GO_Z] = 1.0 - (codes // 4).astype(F32)
    tab[X0], tab[X1], tab[X2] = sweep_factors(own(cx))
    tab[Y0], tab[Y1], tab[Y2] = sweep_factors(own(cy))
    tab[CZ] = own(cz)

    def weights(p, b, held, inverse):
        kept = jnp.exp(row(N_RATE, b) + row(N_SPEED, b) * inverse)
        uu[b, p] = kept * held
        ww[b, p] = (1.0 - kept) * row(WARM_HALF, b)

    def pass_two(r, carry):
        inverse = 1.0 / sp[2 + r]
        fluid = fl[r]
        for b in range(16):
            held = st[b, 2 + r] * fluid
            st[b, 2 + r] = held
            weights(2 + r, b, held, inverse)
        return carry

    lax.fori_loop(0, 8, pass_two, 0)

    halos = []
    for i, (src, dst, strip) in enumerate(((8, 0, right), (2, 10, left))):
        for j, (a, b) in enumerate(
            (
                (sp.at[pl.ds(src, 2)], sp.at[pl.ds(dst, 2)]),
                (st.at[:, pl.ds(src, 2)], st.at[:, pl.ds(dst, 2)]),
            )
        ):
            halos.append(
                pltpu.make_async_remote_copy(
                    a, b, h_send.at[2 * i + j], h_recv.at[2 * i + j], device_id=(m, strip), device_id_type=MESH
                )
            )

    @pl.when(early)
    def _():
        for c in halos:
            c.start()

    depth = lax.broadcasted_iota(jnp.int32, (16, 128), 0)

    def wall_rows(r, carry):
        low = jnp.broadcast_to(wl[0, pl.ds(r, 1), :], (16, 128))
        high = jnp.broadcast_to(wl[1, pl.ds(r, 1), :], (16, 128))
        up_keep[r] = jnp.where((depth == 15) & (high == 0), 0.0, 1.0)
        dn_keep[r] = jnp.where((depth == 0) & (low == 0), 0.0, 1.0)
        bot[r] = jnp.where((depth == 0) & (low == 2), 1.0, 0.0)
        top[r] = jnp.where((depth == 15) & (high == 2), 1.0, 0.0)
        return carry

    lax.fori_loop(0, 8, wall_rows, 0)

    def series():
        order = lax.broadcasted_iota(jnp.int32, (16, 128), 0)
        rest = jnp.exp(-rate)
        powers = jnp.zeros((16, 128), F32)
        term = -rest
        for j in range(RATE_TERMS):
            value = 1.0 - rest if j == 0 else term
            powers = jnp.where(order == j, jnp.broadcast_to(value, (16, 128)), powers)
            term = term * (-speed) * (1.0 / (j + 1))
        weight = warm
        for k in range(TERMS):
            summed = jnp.sum(powers * weight, axis=1, keepdims=True)
            zt[k] = jnp.broadcast_to(summed, (16, 128))
            weight = weight * (bend * bend) * (SCALE * SCALE / ((2 * k + 2) * (2 * k + 3)))

    def moments(p, i):
        inverse = 1.0 / sp[p]
        for k in range(TERMS):
            value = jnp.broadcast_to(zt[k, RATE_TERMS - 1 : RATE_TERMS, :], (16, 128))
            for j in range(RATE_TERMS - 2, -1, -1):
                value = value * inverse + zt[k, j : j + 1, :]
            mu[k, i] = value
        return None

    def iterations(base, slot, count, arrivals):
        for k, recv in arrivals:
            pltpu.make_async_remote_copy(
                part.at[pl.ds(0, count)], got.at[k, pl.ds(slot, count)], rs_send.at[0], recv.at[k],
                device_id=(m, s), device_id_type=MESH,
            ).wait_recv()
        rows = slice(slot, slot + count)
        total = got[0, rows]
        for k in range(1, 8):
            total = total + got[k, rows]
        t = RELAX_WEIGHT * total / mu[0, rows]

        def iterate(_, t):
            q = (t * (1.0 / SCALE)) * (t * (1.0 / SCALE))
            value = mu[TERMS - 1, rows]
            slope = value
            for k in range(TERMS - 2, -1, -1):
                value = value * q + mu[k, rows]
                if k > 0:
                    slope = slope * q + value
            return t - RELAX_WEIGHT * (t * value - total) / (value + 2.0 * q * slope)

        tp[base : base + count] = lax.fori_loop(1, ITERS, iterate, t)

    def t_copy(piece, mode, i):
        _, base, _, count, _ = PIECES[piece]
        return pltpu.make_async_remote_copy(
            tp.at[pl.ds(base, count)], tp.at[pl.ds(base, count)], t_send.at[i], t_recv.at[piece],
            device_id=(mode, s), device_id_type=MESH,
        )

    OWNED = {0: (0, 4), 1: (1,), 2: (2,), 3: (3, 5)}
    pl.when(early)(series)
    for owner in range(4):
        @pl.when(m == owner)
        def _(owner=owner):
            if owner == 0:
                halos[0].wait_recv()
            if owner == 3:
                halos[2].wait_recv()
            lax.fori_loop(0, 3, lambda i, carry: moments(3 * owner + i, i), None)
            for stage, piece in enumerate(OWNED[owner]):
                _, base, slot, count, strip_only = PIECES[piece]
                recv = own_recv if strip_only and count == 1 else rs_recv
                iterations(base, slot, count, [(k, recv) for k in range(8) if k != owner or not strip_only])
                for j in range(1, 4):
                    t_copy(piece, (owner + j) % 4, 8 * stage + j).start()
                if stage == 0:
                    pl.semaphore_wait(l_sem, 4)
                for j in range(4):
                    t_copy(piece, 4 + j, 8 * stage + 4 + j).start()

    @pl.when(late & trails)
    def _():
        for c in halos:
            c.start()

    @pl.when(late & leads)
    def _():
        pl.semaphore_wait(right_sem, 1)
        for c in halos[:2]:
            c.start()
        pl.semaphore_wait(left_sem, 1)
        for c in halos[2:]:
            c.start()

    @pl.when(late & ~leads & ~trails)
    def _():
        for c in halos[2:]:
            c.start()
        pl.semaphore_wait(right_sem, 1)
        for c in halos[:2]:
            c.start()

    def halo_rows(first):
        for p in (first, first + 1):
            inverse = 1.0 / sp[p]
            for b in range(16):
                weights(p, b, st[b, p], inverse)

    def halo_in():
        for i, c in enumerate(halos):
            if i == 0:
                pl.when(m != 0)(c.wait_recv)
            elif i == 2:
                pl.when(m != 3)(c.wait_recv)
            else:
                c.wait_recv()
                halo_rows((0, 10)[i // 2])

    def t_in(piece):
        owner = PIECES[piece][0]
        pl.when(m != owner)(t_copy(piece, owner, 0).wait_recv)

    pl.when(early)(halo_in)
    for piece in range(4):
        t_in(piece)

    def inner_across(b, carry):
        for p in range(2, 10):
            uu[b, p] = relaxed(tp[p], uu[b, p], ww[b, p], row(CURVE, b))
        cells = {p: uu[b, p] for p in range(2, 10)}
        across(b, row, cells, INNER, (up_keep, dn_keep, bot, top), state)
        return carry

    lax.fori_loop(0, 16, inner_across, 0)

    def inner_along(i, carry):
        for j in range(8):
            along(8 * i + j, row, octants[0, 16 * m + 8 * i + j], INNER, fl, state, res)
        return carry

    lax.fori_loop(0, 2, inner_along, 0)
    pl.when(late)(halo_in)
    t_in(4)
    t_in(5)

    for c, when in sends:
        if when is None:
            c.wait_send()
        else:
            pl.when(when)(c.wait_send)
    for c in halos:
        c.wait_send()
    for owner in range(4):
        @pl.when(m == owner)
        def _(owner=owner):
            for stage, piece in enumerate(OWNED[owner]):
                for j in range(1, 8):
                    t_copy(piece, owner, 8 * stage + j).wait_send()


def sweeps(uu, ww, tp, fl, up_keep, dn_keep, bot, top, tab, oc, inner, out, temp_out, state, res, octants, sems):
    signs = pltpu.make_async_copy(oc, octants, sems.at[0])
    signs.start()
    first, count = INNER[0], len(INNER)
    copies = [
        pltpu.make_async_copy(tp.at[pl.ds(2, 8)], temp_out, sems.at[1]),
        pltpu.make_async_copy(inner, out.at[:, pl.ds(first, count)], sems.at[2]),
    ]
    for c in copies:
        c.start()

    def row(table, b):
        return tab[table, pl.ds(b, 1), :]

    def outer_across(b, carry):
        go_x = jnp.broadcast_to(row(GO_X, b), (16, 128)) > 0.5
        cells = {p: uu[b, p] for p in range(2, 10)}
        for p, q in ((1, 10), (0, 11)):
            cells[p] = cells[q] = relaxed(
                jnp.where(go_x, tp[p], tp[q]),
                jnp.where(go_x, uu[b, p], uu[b, q]),
                jnp.where(go_x, ww[b, p], ww[b, q]),
                row(CURVE, b),
            )
        across(b, row, cells, OUTER, (up_keep, dn_keep, bot, top), state)
        return carry

    lax.fori_loop(0, 16, outer_across, 0)
    signs.wait()
    mode = lax.axis_index("mode")

    def outer_along(i, carry):
        for j in range(8):
            along(8 * i + j, row, octants[0, 16 * mode + 8 * i + j], OUTER, fl, state, res)
        for e in range(2):
            pltpu.make_async_copy(
                res.at[pl.ds(8 * i, 8), pl.ds(2 * e, 2)], out.at[pl.ds(8 * i, 8), pl.ds(6 * e, 2)], sems.at[3 + 2 * i + e]
            ).start()
        return carry

    for i in range(2):
        outer_along(i, None)
    for i in range(2):
        for e in range(2):
            copies.append(
                pltpu.make_async_copy(
                    res.at[pl.ds(8 * i, 8), pl.ds(2 * e, 2)], out.at[pl.ds(8 * i, 8), pl.ds(6 * e, 2)], sems.at[3 + 2 * i + e]
                )
            )
    for c in copies:
        c.wait()


def solution(mesh):
    space = mesh.shape["space"]

    def local(energy, void, spacing, walls, octant, warmth, curve, umklapp, isotope, courant):
        flat = lambda v: v.reshape(1, 128)
        vmem = pl.BlockSpec(memory_space=pltpu.VMEM)
        dma = pltpu.SemaphoreType.DMA
        regular = pltpu.SemaphoreType.REGULAR
        held, quarter = (16, 12, 16, 128), (16, 4, 16, 128)
        cells = spacing.shape
        sums = pl.pallas_call(
            functools.partial(kernel, space),
            out_shape=(
                [pltpu.VMEM(held, F32)] * 2
                + [pltpu.VMEM((12, 16, 128), F32)]
                + [pltpu.VMEM(cells, F32)] * 5
                + [pltpu.VMEM((14, 16, 128), F32), pltpu.VMEM((1, 128), jnp.int32), pltpu.VMEM(quarter, F32)]
            ),
            in_specs=[pl.BlockSpec(memory_space=pltpu.HBM)] * 10,
            out_specs=[vmem] * 11,
            scratch_shapes=[
                pltpu.VMEM(quarter, F32),
                pltpu.SMEM((1, 128), jnp.int32),
                pltpu.VMEM(held, F32),
                pltpu.VMEM((12, 16, 128), F32),
                pltpu.VMEM(cells, jnp.int32),
                pltpu.VMEM((2, 8, 128), jnp.int32),
                pltpu.VMEM((32, 128), F32),
                pltpu.VMEM((3, 128), F32),
                pltpu.VMEM(cells, F32),
                pltpu.VMEM((8, 3, 16, 128), F32),
                pltpu.VMEM((TERMS, 3, 16, 128), F32),
                pltpu.VMEM((TERMS, 16, 128), F32),
                dma((2,)),
                dma((10,)),
                dma((6,)),
                dma((8,)),
                dma((8,)),
                dma((16,)),
                dma((6,)),
                dma((4,)),
                dma((4,)),
                regular,
                regular,
                regular,
            ],
            compiler_params=pltpu.CompilerParams(
                collective_id=0, has_side_effects=True, vmem_limit_bytes=24 * 1024 * 1024
            ),
        )(
            *[
                pltpu.with_memory_space_constraint(v, pltpu.HBM)
                for v in (
                    energy, void, spacing, walls, flat(octant), flat(warmth), flat(curve), flat(umklapp),
                    flat(isotope), courant,
                )
            ]
        )
        return pl.pallas_call(
            sweeps,
            out_shape=(pltpu.HBM(energy.shape, F32), pltpu.HBM(cells, F32)),
            in_specs=[vmem] * 11,
            out_specs=[pl.BlockSpec(memory_space=pltpu.HBM)] * 2,
            scratch_shapes=[
                pltpu.VMEM(quarter, F32),
                pltpu.VMEM(quarter, F32),
                pltpu.SMEM((1, 128), jnp.int32),
                dma((7,)),
            ],
            compiler_params=pltpu.CompilerParams(vmem_limit_bytes=24 * 1024 * 1024),
        )(*sums)

    in_specs = (
        P("mode", "space", None, None),
        P("space", None, None),
        P("space", None, None),
        P(None, "space", None),
        P(),
        P(),
        P(),
        P(),
        P(),
        P(),
    )
    out_specs = (P("mode", "space", None, None), P("space", None, None))
    return jax.shard_map(local, mesh=mesh, in_specs=in_specs, out_specs=out_specs, check_vma=False)
```

time: 29.7 us -> 24.3 us (0.82)
  the two profiles are of different devices: /device:TPU:136 before, /device:TPU:38 now
where the time goes in v2:
time: 24.3 us; the launch traced here: 24.1 us
  Pallas kernels  23.4 us (96%)
  between operations  0.64 us (3%)
    pallas_call x1, Pallas kernels, local(): pl.pallas_call(functools.partial(kernel, space), out_shape=[pltpu.VMEM(he...  21.7 us
    pallas_call x1, Pallas kernels, local(): pl.pallas_call(sweeps, out_shape=(pltpu.HBM(energy.shape, F32), pltpu.HBM...  1.72 us

profile of v2, /device:TPU:38, one launch (start us, length us, event | category | flops | bytes accessed | tf_op | source)
XLA Modules:
  0.0 24.1 jit_solution(13629832652327602619)
XLA Ops:
  0.6 21.7 %shard_map.113 = (f32[16,12,16,128]{3,2,1,0:T(8,128)S(1)}, f32[16,12,16,128]{3,2,1,0:T(8,128)S(1)}, f32[12,16,128]{2,1,0:T(8,128)S(1)}, f32[8,16,128]{2,1,0:T(8,...) custom-call(f32[16,8,16,128]{3,2,1,0:T(8,128)} %energy.1, ...), custom_call_target="tpu_custom_call" | custom-call | tf_op jit(solution)/shard_map/pallas_call | solution.py:499
  22.3 1.7 %shard_map.114 = (f32[16,8,16,128]{3,2,1,0:T(8,128)}, f32[8,16,128]{2,1,0:T(8,128)}) custom-call(f32[16,12,16,128]{3,2,1,0:T(8,128)S(1)} %get-tuple-element.13.uu, f32[16,12,16,128]{3,2,1,0:T(8,128)S(1)} %get-tuple-element.14.ww, f32[12,16,128]{2,1,0:T(8,128)S(1)} %get-tuple-element.15.tp, f32[8,16,128]{2,1,0:T(8,128)S(1)} %get-tuple-element.16.fl, ...), custom_call_target="tpu_custom_call" | custom-call | tf_op jit(solution)/shard_map/pallas_call | solution.py:547

commit v3 on v2

--- a/solution.py
+++ b/solution.py
@@ -25,6 +25,7 @@
     return 1.0 - 1.5 * c + 0.5 * c * c, 2.0 * c - c * c, 0.5 * c * c - 0.5 * c
 
 
+OWNERS = (1, 2, 0, 3)
 PIECES = ((0, 2, 2, 1, True), (1, 3, 0, 3, True), (2, 6, 0, 3, True), (3, 9, 0, 1, True), (0, 0, 0, 2, False), (3, 10, 1, 2, False))
 INNER, OUTER = (2, 3, 4, 5), (0, 1, 6, 7)
 
@@ -64,7 +65,7 @@
     space,
     energy, void, spacing, walls, octant, warmth, curve, umklapp, isotope, courant,
     uu, ww, tp, fl, up_keep, dn_keep, bot, top, tab, oc, res,
-    state, octants, st, sp, vd, wl, pv, cr, part, got, mu, zt,
+    state, octants, st, sp, vd, wl, pv, cr, part, got, mu, mu_slope, zt,
     in_sem, small_sem, rs_send, rs_recv, own_recv, t_send, t_recv, h_send, h_recv, l_sem, left_sem, right_sem,
 ):
     m, s = lax.axis_index("mode"), lax.axis_index("space")
@@ -75,6 +76,30 @@
 
     def signal(sem, mode, strip):
         pl.semaphore_signal(sem, inc=1, device_id=(mode, strip), device_id_type=MESH)
+
+    barrier = pltpu.get_barrier_semaphore()
+
+    @pl.when(early)
+    def _():
+        for j in range(4):
+            signal(barrier, 4 + j, s)
+
+    @pl.when(m == OWNERS[0])
+    def _():
+        for k in range(8):
+            signal(barrier, 7 - k, left)
+
+    @pl.when(m == OWNERS[3])
+    def _():
+        for k in range(8):
+            signal(barrier, 7 - k, right)
+
+    @pl.when(early)
+    def _():
+        for j in range(1, 4):
+            signal(barrier, lax.rem(m + j, 4), s)
+        for strip in (left, right):
+            signal(barrier, y, strip)
 
     small = [
         pltpu.make_async_copy(src, dst, small_sem.at[i])
@@ -106,25 +131,6 @@
     for c in small[5:]:
         c.start()
 
-    barrier = pltpu.get_barrier_semaphore()
-
-    @pl.when(early)
-    def _():
-        for j in range(1, 8):
-            signal(barrier, lax.rem(m + j, 8), s)
-        for strip in (left, right):
-            signal(barrier, y, strip)
-
-    @pl.when(m == 0)
-    def _():
-        for k in range(8):
-            signal(barrier, k, left)
-
-    @pl.when(m == 3)
-    def _():
-        for k in range(8):
-            signal(barrier, k, right)
-
     place = lax.rem(s, RUN)
     leads, trails = place == 0, place == RUN - 1
 
@@ -151,21 +157,6 @@
     speed = jnp.sqrt(cx * cx + cy * cy + cz * cz)
     tab[N_RATE] = own(-rate)
     tab[N_SPEED] = own(-speed)
-
-    pl.semaphore_wait(barrier, jnp.where(early, 7, 7 + trails.astype(jnp.int32) - leads.astype(jnp.int32)))
-
-    @pl.when(late)
-    def _():
-        for k in range(4):
-            signal(l_sem, k, s)
-
-    @pl.when(late & ~leads)
-    def _():
-        signal(right_sem, m, left)
-
-    @pl.when(late & trails)
-    def _():
-        signal(left_sem, m, right)
 
     def row(table, b):
         return tab[table, pl.ds(b, 1), :]
@@ -198,18 +189,34 @@
         else:
             pl.when(when)(c.start)
 
-    loads[0].wait()
-    lax.fori_loop(0, 4, pass_one, 0)
-    send(0, 2, 1, 3, left, 0, rs_recv, None)
-    send(1, 3, 0, 1, s, 1, rs_recv, m != 1)
-    send(0, 1, 2, 0, s, 2, own_recv, m != 0)
-    loads[1].wait()
-    lax.fori_loop(4, 8, pass_one, 0)
-    send(6, 2, 0, 0, right, 3, rs_recv, None)
-    send(4, 3, 0, 2, s, 4, rs_recv, m != 2)
-    send(7, 1, 0, 3, s, 5, own_recv, m != 3)
-
-    for owner, slot, first, count in ((0, 2, 0, 1), (1, 0, 1, 3), (2, 0, 4, 3), (3, 0, 7, 1)):
+    for i in range(2):
+        loads[i].wait()
+        lax.fori_loop(4 * i, 4 * i + 4, pass_one, 0)
+
+    pl.semaphore_wait(barrier, jnp.where(early, 7, 7 + trails.astype(jnp.int32) - leads.astype(jnp.int32)))
+    send(6, 2, 0, OWNERS[0], right, 3, rs_recv, None)
+    send(0, 2, 1, OWNERS[3], left, 0, rs_recv, None)
+    send(1, 3, 0, OWNERS[1], s, 1, rs_recv, m != OWNERS[1])
+    send(4, 3, 0, OWNERS[2], s, 4, rs_recv, m != OWNERS[2])
+    send(0, 1, 2, OWNERS[0], s, 2, own_recv, m != OWNERS[0])
+    send(7, 1, 0, OWNERS[3], s, 5, own_recv, m != OWNERS[3])
+
+    @pl.when(late)
+    def _():
+        for k in range(4):
+            signal(l_sem, k, s)
+
+    @pl.when(late & ~leads)
+    def _():
+        signal(right_sem, m, left)
+
+    @pl.when(late & trails)
+    def _():
+        signal(left_sem, m, right)
+
+    for role, slot, first, count in ((0, 2, 0, 1), (1, 0, 1, 3), (2, 0, 4, 3), (3, 0, 7, 1)):
+        owner = OWNERS[role]
+
         @pl.when(m == owner)
         def _(owner=owner, slot=slot, first=first, count=count):
             got[owner, slot : slot + count] = part[first : first + count]
@@ -299,6 +306,7 @@
             for j in range(RATE_TERMS - 2, -1, -1):
                 value = value * inverse + zt[k, j : j + 1, :]
             mu[k, i] = value
+            mu_slope[k, i] = value * (2.0 * k + 1.0)
         return None
 
     def iterations(base, slot, count, arrivals):
@@ -315,13 +323,16 @@
 
         def iterate(_, t):
             q = (t * (1.0 / SCALE)) * (t * (1.0 / SCALE))
-            value = mu[TERMS - 1, rows]
-            slope = value
-            for k in range(TERMS - 2, -1, -1):
-                value = value * q + mu[k, rows]
-                if k > 0:
-                    slope = slope * q + value
-            return t - RELAX_WEIGHT * (t * value - total) / (value + 2.0 * q * slope)
+            square = q * q
+
+            def series_at(table):
+                even, odd = table[TERMS - 2, rows], table[TERMS - 1, rows]
+                for k in range(TERMS - 4, -1, -2):
+                    even = even * square + table[k, rows]
+                    odd = odd * square + table[k + 1, rows]
+                return even + q * odd
+
+            return t - RELAX_WEIGHT * (t * series_at(mu) - total) / series_at(mu_slope)
 
         tp[base : base + count] = lax.fori_loop(1, ITERS, iterate, t)
 
@@ -334,15 +345,15 @@
 
     OWNED = {0: (0, 4), 1: (1,), 2: (2,), 3: (3, 5)}
     pl.when(early)(series)
-    for owner in range(4):
+    for role, owner in enumerate(OWNERS):
         @pl.when(m == owner)
-        def _(owner=owner):
-            if owner == 0:
+        def _(role=role, owner=owner):
+            if role == 0:
                 halos[0].wait_recv()
-            if owner == 3:
+            if role == 3:
                 halos[2].wait_recv()
-            lax.fori_loop(0, 3, lambda i, carry: moments(3 * owner + i, i), None)
-            for stage, piece in enumerate(OWNED[owner]):
+            lax.fori_loop(0, 3, lambda i, carry: moments(3 * role + i, i), None)
+            for stage, piece in enumerate(OWNED[role]):
                 _, base, slot, count, strip_only = PIECES[piece]
                 recv = own_recv if strip_only and count == 1 else rs_recv
                 iterations(base, slot, count, [(k, recv) for k in range(8) if k != owner or not strip_only])
@@ -384,15 +395,15 @@
     def halo_in():
         for i, c in enumerate(halos):
             if i == 0:
-                pl.when(m != 0)(c.wait_recv)
+                pl.when(m != OWNERS[0])(c.wait_recv)
             elif i == 2:
-                pl.when(m != 3)(c.wait_recv)
+                pl.when(m != OWNERS[3])(c.wait_recv)
             else:
                 c.wait_recv()
                 halo_rows((0, 10)[i // 2])
 
     def t_in(piece):
-        owner = PIECES[piece][0]
+        owner = OWNERS[PIECES[piece][0]]
         pl.when(m != owner)(t_copy(piece, owner, 0).wait_recv)
 
     pl.when(early)(halo_in)
@@ -425,10 +436,10 @@
             pl.when(when)(c.wait_send)
     for c in halos:
         c.wait_send()
-    for owner in range(4):
+    for role, owner in enumerate(OWNERS):
         @pl.when(m == owner)
-        def _(owner=owner):
-            for stage, piece in enumerate(OWNED[owner]):
+        def _(role=role, owner=owner):
+            for stage, piece in enumerate(OWNED[role]):
                 for j in range(1, 8):
                     t_copy(piece, owner, 8 * stage + j).wait_send()
 
@@ -517,6 +528,7 @@
                 pltpu.VMEM((3, 128), F32),
                 pltpu.VMEM(cells, F32),
                 pltpu.VMEM((8, 3, 16, 128), F32),
+                pltpu.VMEM((TERMS, 3, 16, 128), F32),
                 pltpu.VMEM((TERMS, 3, 16, 128), F32),
                 pltpu.VMEM((TERMS, 16, 128), F32),
                 dma((2,)),

time: 24.3 us -> 24.1 us (level)
  no operation moved by 1% of the time
where the time goes in v3:
time: 24.1 us; the launch traced here: 23.9 us
  Pallas kernels  23.3 us (97%)
  between operations  0.64 us (3%)
    pallas_call x1, Pallas kernels, local(): pl.pallas_call(functools.partial(kernel, space), out_shape=[pltpu.VMEM(he...  21.6 us
    pallas_call x1, Pallas kernels, local(): pl.pallas_call(sweeps, out_shape=(pltpu.HBM(energy.shape, F32), pltpu.HBM...  1.72 us

profile of v3, /device:TPU:38, one launch (start us, length us, event | category | flops | bytes accessed | tf_op | source)
XLA Modules:
  0.0 23.9 jit_solution(3512553227096434962)
XLA Ops:
  0.6 21.6 %shard_map.113 = (f32[16,12,16,128]{3,2,1,0:T(8,128)S(1)}, f32[16,12,16,128]{3,2,1,0:T(8,128)S(1)}, f32[12,16,128]{2,1,0:T(8,128)S(1)}, f32[8,16,128]{2,1,0:T(8,...) custom-call(f32[16,8,16,128]{3,2,1,0:T(8,128)} %energy.1, ...), custom_call_target="tpu_custom_call" | custom-call | tf_op jit(solution)/shard_map/pallas_call | solution.py:510
  22.2 1.7 %shard_map.114 = (f32[16,8,16,128]{3,2,1,0:T(8,128)}, f32[8,16,128]{2,1,0:T(8,128)}) custom-call(f32[16,12,16,128]{3,2,1,0:T(8,128)S(1)} %get-tuple-element.13.uu, f32[16,12,16,128]{3,2,1,0:T(8,128)S(1)} %get-tuple-element.14.ww, f32[12,16,128]{2,1,0:T(8,128)S(1)} %get-tuple-element.15.tp, f32[8,16,128]{2,1,0:T(8,128)S(1)} %get-tuple-element.16.fl, ...), custom_call_target="tpu_custom_call" | custom-call | tf_op jit(solution)/shard_map/pallas_call | solution.py:559

commit v4 on v3

--- a/solution.py
+++ b/solution.py
@@ -214,43 +214,12 @@
     def _():
         signal(left_sem, m, right)
 
-    for role, slot, first, count in ((0, 2, 0, 1), (1, 0, 1, 3), (2, 0, 4, 3), (3, 0, 7, 1)):
-        owner = OWNERS[role]
-
-        @pl.when(m == owner)
-        def _(owner=owner, slot=slot, first=first, count=count):
-            got[owner, slot : slot + count] = part[first : first + count]
-
-    for c in small[5:]:
-        c.wait()
-
-    warm, bend = pv[16:17, :], pv[24:25, :]
-    own_warm, own_bend = own(warm), own(bend)
-    tab[WARM_HALF] = 0.5 * own_warm / own_bend
-    tab[CURVE] = own_bend * (1.0 / math.log(2.0))
-    tab[HOT] = (0.5 * own_warm / own_bend) * (jnp.exp(own_bend * HOT_WALL) - jnp.exp(-own_bend * HOT_WALL))
-    codes = own(oc[0:1, :].astype(F32)).astype(jnp.int32)
-    tab[GO_X] = 1.0 - (codes & 1).astype(F32)
-    tab[GO_Z] = 1.0 - (codes // 4).astype(F32)
-    tab[X0], tab[X1], tab[X2] = sweep_factors(own(cx))
-    tab[Y0], tab[Y1], tab[Y2] = sweep_factors(own(cy))
-    tab[CZ] = own(cz)
-
-    def weights(p, b, held, inverse):
-        kept = jnp.exp(row(N_RATE, b) + row(N_SPEED, b) * inverse)
-        uu[b, p] = kept * held
-        ww[b, p] = (1.0 - kept) * row(WARM_HALF, b)
-
-    def pass_two(r, carry):
-        inverse = 1.0 / sp[2 + r]
-        fluid = fl[r]
-        for b in range(16):
-            held = st[b, 2 + r] * fluid
-            st[b, 2 + r] = held
-            weights(2 + r, b, held, inverse)
-        return carry
-
-    lax.fori_loop(0, 8, pass_two, 0)
+    def edges(b, carry):
+        for r in OUTER:
+            st[b, 2 + r] = st[b, 2 + r] * fl[r]
+        return carry
+
+    lax.fori_loop(0, 16, edges, 0)
 
     halos = []
     for i, (src, dst, strip) in enumerate(((8, 0, right), (2, 10, left))):
@@ -266,10 +235,51 @@
                 )
             )
 
-    @pl.when(early)
-    def _():
-        for c in halos:
+    @pl.when(early | trails)
+    def _():
+        for c in halos[:2]:
             c.start()
+
+    @pl.when(early | ~leads)
+    def _():
+        for c in halos[2:]:
+            c.start()
+
+    for role, slot, first, count in ((0, 2, 0, 1), (1, 0, 1, 3), (2, 0, 4, 3), (3, 0, 7, 1)):
+        owner = OWNERS[role]
+
+        @pl.when(m == owner)
+        def _(owner=owner, slot=slot, first=first, count=count):
+            got[owner, slot : slot + count] = part[first : first + count]
+
+    for c in small[5:]:
+        c.wait()
+
+    warm, bend = pv[16:17, :], pv[24:25, :]
+    own_warm, own_bend = own(warm), own(bend)
+    tab[WARM_HALF] = 0.5 * own_warm / own_bend
+    tab[CURVE] = own_bend * (1.0 / math.log(2.0))
+    tab[HOT] = (0.5 * own_warm / own_bend) * (jnp.exp(own_bend * HOT_WALL) - jnp.exp(-own_bend * HOT_WALL))
+    codes = own(oc[0:1, :].astype(F32)).astype(jnp.int32)
+    tab[GO_X] = 1.0 - (codes & 1).astype(F32)
+    tab[GO_Z] = 1.0 - (codes // 4).astype(F32)
+    tab[X0], tab[X1], tab[X2] = sweep_factors(own(cx))
+    tab[Y0], tab[Y1], tab[Y2] = sweep_factors(own(cy))
+    tab[CZ] = own(cz)
+
+    def weights(p, b, held, inverse):
+        kept = jnp.exp(row(N_RATE, b) + row(N_SPEED, b) * inverse)
+        uu[b, p] = kept * held
+        ww[b, p] = (1.0 - kept) * row(WARM_HALF, b)
+
+    def pass_two(r, carry):
+        inverse = 1.0 / sp[2 + r]
+        fluid = fl[r]
+        for b in range(16):
+            weights(2 + r, b, st[b, 2 + r] * fluid, inverse)
+        return carry
+
+    lax.fori_loop(0, 8, pass_two, 0)
 
     depth = lax.broadcasted_iota(jnp.int32, (16, 128), 0)
 
@@ -364,26 +374,16 @@
                 for j in range(4):
                     t_copy(piece, 4 + j, 8 * stage + 4 + j).start()
 
-    @pl.when(late & trails)
-    def _():
-        for c in halos:
-            c.start()
-
-    @pl.when(late & leads)
+    @pl.when(late & ~trails)
     def _():
         pl.semaphore_wait(right_sem, 1)
         for c in halos[:2]:
             c.start()
+
+    @pl.when(late & leads)
+    def _():
         pl.semaphore_wait(left_sem, 1)
         for c in halos[2:]:
-            c.start()
-
-    @pl.when(late & ~leads & ~trails)
-    def _():
-        for c in halos[2:]:
-            c.start()
-        pl.semaphore_wait(right_sem, 1)
-        for c in halos[:2]:
             c.start()
 
     def halo_rows(first):
@@ -417,7 +417,7 @@
         across(b, row, cells, INNER, (up_keep, dn_keep, bot, top), state)
         return carry
 
-    lax.fori_loop(0, 16, inner_across, 0)
+    lax.fori_loop(0, 16, inner_across, 0, unroll=4)
 
     def inner_along(i, carry):
         for j in range(8):
@@ -471,7 +471,7 @@
         across(b, row, cells, OUTER, (up_keep, dn_keep, bot, top), state)
         return carry
 
-    lax.fori_loop(0, 16, outer_across, 0)
+    lax.fori_loop(0, 16, outer_across, 0, unroll=2)
     signs.wait()
     mode = lax.axis_index("mode")
 

time: 24.1 us -> 23.9 us (level)
  no operation moved by 1% of the time
where the time goes in v4:
time: 23.9 us; the launch traced here: 23.8 us
  Pallas kernels  23.1 us (97%)
  between operations  0.64 us (3%)
    pallas_call x1, Pallas kernels, local(): pl.pallas_call(functools.partial(kernel, space), out_shape=[pltpu.VMEM(he...  21.5 us
    pallas_call x1, Pallas kernels, local(): pl.pallas_call(sweeps, out_shape=(pltpu.HBM(energy.shape, F32), pltpu.HBM...  1.66 us

profile of v4, /device:TPU:38, one launch (start us, length us, event | category | flops | bytes accessed | tf_op | source)
XLA Modules:
  0.0 23.8 jit_solution(7003848319310499111)
XLA Ops:
  0.6 21.5 %shard_map.113 = (f32[16,12,16,128]{3,2,1,0:T(8,128)S(1)}, f32[16,12,16,128]{3,2,1,0:T(8,128)S(1)}, f32[12,16,128]{2,1,0:T(8,128)S(1)}, f32[8,16,128]{2,1,0:T(8,...) custom-call(f32[16,8,16,128]{3,2,1,0:T(8,128)} %energy.1, ...), custom_call_target="tpu_custom_call" | custom-call | tf_op jit(solution)/shard_map/pallas_call | solution.py:510
  22.1 1.7 %shard_map.114 = (f32[16,8,16,128]{3,2,1,0:T(8,128)}, f32[8,16,128]{2,1,0:T(8,128)}) custom-call(f32[16,12,16,128]{3,2,1,0:T(8,128)S(1)} %get-tuple-element.13.uu, f32[16,12,16,128]{3,2,1,0:T(8,128)S(1)} %get-tuple-element.14.ww, f32[12,16,128]{2,1,0:T(8,128)S(1)} %get-tuple-element.15.tp, f32[8,16,128]{2,1,0:T(8,128)S(1)} %get-tuple-element.16.fl, ...), custom_call_target="tpu_custom_call" | custom-call | tf_op jit(solution)/shard_map/pallas_call | solution.py:559

commit v5 on v4

--- a/solution.py
+++ b/solution.py
@@ -476,21 +476,21 @@
     mode = lax.axis_index("mode")
 
     def outer_along(i, carry):
-        for j in range(8):
-            along(8 * i + j, row, octants[0, 16 * mode + 8 * i + j], OUTER, fl, state, res)
+        for j in range(4):
+            along(4 * i + j, row, octants[0, 16 * mode + 4 * i + j], OUTER, fl, state, res)
         for e in range(2):
             pltpu.make_async_copy(
-                res.at[pl.ds(8 * i, 8), pl.ds(2 * e, 2)], out.at[pl.ds(8 * i, 8), pl.ds(6 * e, 2)], sems.at[3 + 2 * i + e]
+                res.at[pl.ds(4 * i, 4), pl.ds(2 * e, 2)], out.at[pl.ds(4 * i, 4), pl.ds(6 * e, 2)], sems.at[3 + 2 * i + e]
             ).start()
         return carry
 
-    for i in range(2):
+    for i in range(4):
         outer_along(i, None)
-    for i in range(2):
+    for i in range(4):
         for e in range(2):
             copies.append(
                 pltpu.make_async_copy(
-                    res.at[pl.ds(8 * i, 8), pl.ds(2 * e, 2)], out.at[pl.ds(8 * i, 8), pl.ds(6 * e, 2)], sems.at[3 + 2 * i + e]
+                    res.at[pl.ds(4 * i, 4), pl.ds(2 * e, 2)], out.at[pl.ds(4 * i, 4), pl.ds(6 * e, 2)], sems.at[3 + 2 * i + e]
                 )
             )
     for c in copies:
@@ -565,7 +565,7 @@
                 pltpu.VMEM(quarter, F32),
                 pltpu.VMEM(quarter, F32),
                 pltpu.SMEM((1, 128), jnp.int32),
-                dma((7,)),
+                dma((11,)),
             ],
             compiler_params=pltpu.CompilerParams(vmem_limit_bytes=24 * 1024 * 1024),
         )(*sums)

time: 23.9 us -> 23.9 us (level)
  no operation moved by 1% of the time
where the time goes in v5:
time: 23.9 us; the launch traced here: 23.8 us
  Pallas kernels  23.1 us (97%)
  between operations  0.64 us (3%)
    pallas_call x1, Pallas kernels, local(): pl.pallas_call(functools.partial(kernel, space), out_shape=[pltpu.VMEM(he...  21.5 us
    pallas_call x1, Pallas kernels, local(): pl.pallas_call(sweeps, out_shape=(pltpu.HBM(energy.shape, F32), pltpu.HBM...  1.65 us

profile of v5, /device:TPU:38, one launch (start us, length us, event | category | flops | bytes accessed | tf_op | source)
XLA Modules:
  0.0 23.8 jit_solution(3499686193783888932)
XLA Ops:
  0.6 21.5 %shard_map.113 = (f32[16,12,16,128]{3,2,1,0:T(8,128)S(1)}, f32[16,12,16,128]{3,2,1,0:T(8,128)S(1)}, f32[12,16,128]{2,1,0:T(8,128)S(1)}, f32[8,16,128]{2,1,0:T(8,...) custom-call(f32[16,8,16,128]{3,2,1,0:T(8,128)} %energy.1, ...), custom_call_target="tpu_custom_call" | custom-call | tf_op jit(solution)/shard_map/pallas_call | solution.py:510
  22.1 1.6 %shard_map.114 = (f32[16,8,16,128]{3,2,1,0:T(8,128)}, f32[8,16,128]{2,1,0:T(8,128)}) custom-call(f32[16,12,16,128]{3,2,1,0:T(8,128)S(1)} %get-tuple-element.13.uu, f32[16,12,16,128]{3,2,1,0:T(8,128)S(1)} %get-tuple-element.14.ww, f32[12,16,128]{2,1,0:T(8,128)S(1)} %get-tuple-element.15.tp, f32[8,16,128]{2,1,0:T(8,128)S(1)} %get-tuple-element.16.fl, ...), custom_call_target="tpu_custom_call" | custom-call | tf_op jit(solution)/shard_map/pallas_call | solution.py:559

commit v6 on v4

--- a/solution.py
+++ b/solution.py
@@ -367,12 +367,12 @@
                 _, base, slot, count, strip_only = PIECES[piece]
                 recv = own_recv if strip_only and count == 1 else rs_recv
                 iterations(base, slot, count, [(k, recv) for k in range(8) if k != owner or not strip_only])
-                for j in range(1, 4):
+                for j in (2, 1, 3):
                     t_copy(piece, (owner + j) % 4, 8 * stage + j).start()
                 if stage == 0:
                     pl.semaphore_wait(l_sem, 4)
-                for j in range(4):
-                    t_copy(piece, 4 + j, 8 * stage + 4 + j).start()
+                for j in (2, 1, 3, 0):
+                    t_copy(piece, 4 + (owner + j) % 4, 8 * stage + 4 + j).start()
 
     @pl.when(late & ~trails)
     def _():

time: 23.9 us -> 23.7 us (level)
  Pallas kernels: 23.1 us -> 22.8 us
    pallas_call x1, Pallas kernels: 21.5 us -> 21.2 us  [local(): pl.pallas_call(functools.partial(kernel, space), out_shape=[pltpu.VMEM(he...]
where the time goes in v6:
time: 23.7 us; the launch traced here: 23.5 us
  Pallas kernels  22.8 us (96%)
  between operations  0.64 us (3%)
    pallas_call x1, Pallas kernels, local(): pl.pallas_call(functools.partial(kernel, space), out_shape=[pltpu.VMEM(he...  21.2 us
    pallas_call x1, Pallas kernels, local(): pl.pallas_call(sweeps, out_shape=(pltpu.HBM(energy.shape, F32), pltpu.HBM...  1.66 us

profile of v6, /device:TPU:38, one launch (start us, length us, event | category | flops | bytes accessed | tf_op | source)
XLA Modules:
  0.0 23.5 jit_solution(11293800703059930193)
XLA Ops:
  0.6 21.2 %shard_map.113 = (f32[16,12,16,128]{3,2,1,0:T(8,128)S(1)}, f32[16,12,16,128]{3,2,1,0:T(8,128)S(1)}, f32[12,16,128]{2,1,0:T(8,128)S(1)}, f32[8,16,128]{2,1,0:T(8,...) custom-call(f32[16,8,16,128]{3,2,1,0:T(8,128)} %energy.1, ...), custom_call_target="tpu_custom_call" | custom-call | tf_op jit(solution)/shard_map/pallas_call | solution.py:510
  21.8 1.7 %shard_map.114 = (f32[16,8,16,128]{3,2,1,0:T(8,128)}, f32[8,16,128]{2,1,0:T(8,128)}) custom-call(f32[16,12,16,128]{3,2,1,0:T(8,128)S(1)} %get-tuple-element.13.uu, f32[16,12,16,128]{3,2,1,0:T(8,128)S(1)} %get-tuple-element.14.ww, f32[12,16,128]{2,1,0:T(8,128)S(1)} %get-tuple-element.15.tp, f32[8,16,128]{2,1,0:T(8,128)S(1)} %get-tuple-element.16.fl, ...), custom_call_target="tpu_custom_call" | custom-call | tf_op jit(solution)/shard_map/pallas_call | solution.py:559
